TPU v7x, 32 devices: a whole 2x2x4 slice. The times are simulated.
32 devices in a mesh: storm: 2 (over x), dom: 16 (over z, y, core).
Axes of the slice: x: 2, y: 2, z: 4, core: 2. Of those that a mesh axis runs over, the one named last changes fastest.
Arguments:
- eta_start: float32 [2048, 128], P(('storm', 'dom')), parts along dimension 0, may hold values from -4 to 4
- forcing: float32 [4, 2048, 128], P(None, ('storm', 'dom')), parts along dimension 1, may hold values from -3 to 3
- diagonal: float32 [1024, 128], P('dom'), may hold values from 1 to 2
- coupling: bfloat16 [1024, 4, 128, 128], P('dom'), may hold values from -0.5 to 0.5
- neighbours: int32 [1024, 4], P('dom'), may hold values from 0 to 127, as said below
- wet: int32 [1024, 128], P('dom'), may hold values 0 or 1
- grid_nodes: int32 [3, 131072], P(None, 'dom'), may hold values from 0 to 8191
- grid_weights: float32 [3, 131072], P(None, 'dom'), may hold values from 0 to 1, as said below
Outputs:
- return_level: float32 [262144], P(('storm', 'dom')), parts along dimension 0
- grid_final: float32 [262144], P(('storm', 'dom')), parts along dimension 0
There are 2 independent parts, one for each index of `storm`. A program takes and returns all parts, laid end to end along the dimension named above; an argument that names none is the same for every part. Nothing has to cross between parts.
Inputs may be any that keep to these rules, and one draw needn't show every extreme that they name: `neighbours`: entries index the 32 blocks before a partition's own 64, those, and the 32 after, counted from 0; slot 0 of a row is the row's own block; the slots of a row name distinct blocks. `grid_weights`: Nonnegative; the three weights of a cell sum to one.
All inputs are finite; a program needn't handle non-finite values. No bound on the sum of `wet` on one device may be relied on, other than what follows from the above.
Results may differ from a plain program's by a relative error of at most 0.0003.
Values may be sent and summed in bfloat16 or wider, within the bound.
A program may use at most 64 MiB of HBM per device.

v0:
```python
import jax
import jax.numpy as jnp
from jax import lax
from jax.sharding import PartitionSpec as P

STEPS = 4
SWEEPS = 8


def padded_2(block, sides, width):
    for axis, dim in sides:
        count = lax.axis_size(axis)
        forward = [(i, i + 1) for i in range(count - 1)]
        backward = [(target, source) for source, target in forward]
        low = lax.ppermute(
            lax.slice_in_dim(block, block.shape[dim] - width, None, axis=dim), axis, forward
        )
        high = lax.ppermute(lax.slice_in_dim(block, 0, width, axis=dim), axis, backward)
        block = jnp.concatenate([low, block, high], axis=dim)
    return block


def interpolate(strip_values, grid_nodes, grid_weights):
    flattened = strip_values.reshape(-1)
    sampled = flattened[grid_nodes]
    return jnp.sum(grid_weights * sampled, axis=0)


def couple(blocks, nearby):
    return jnp.einsum(
        "bsij,bsj->bi",
        blocks,
        nearby,
        precision=lax.Precision.HIGHEST,
        preferred_element_type=jnp.float32,
    )


def local(eta_start, forcing, diagonal, coupling, neighbours, wet, grid_nodes, grid_weights):
    blocks_here = coupling.shape[0]
    margin_rows = blocks_here // 2
    domains = lax.axis_size("dom")
    wet_share = wet.astype(jnp.float32)
    surface = eta_start
    snapshots = []
    for step_index in range(STEPS):
        source = diagonal * surface + forcing[step_index]
        for sweep_index in range(SWEEPS):
            padded = padded_2(surface, (("dom", 0),), margin_rows)
            coupled = couple(coupling, padded[neighbours])
            surface = wet_share * (source - coupled) / diagonal
        snapshots.append(surface)
    stacked = jnp.stack(snapshots).reshape(len(snapshots), domains, -1)
    received = lax.all_to_all(stacked, "dom", split_axis=1, concat_axis=1, tiled=True)
    highest = jnp.max(received, axis=0)
    latest = received[-1]
    return (
        interpolate(highest, grid_nodes, grid_weights),
        interpolate(latest, grid_nodes, grid_weights),
    )


def solution(mesh):
    in_specs = (
        P(("storm", "dom"), None),
        P(None, ("storm", "dom"), None),
        P("dom", None),
        P("dom", None, None, None),
        P("dom", None),
        P("dom", None),
        P(None, "dom"),
        P(None, "dom"),
    )
    out_specs = (P(("storm", "dom")), P(("storm", "dom")))
    return jax.shard_map(local, mesh=mesh, in_specs=in_specs, out_specs=out_specs, check_vma=False)
```

profile of v0, /device:TPU:0, one launch (start us, length us, event | category | flops | bytes accessed | tf_op | source)
XLA Modules:
  0.0 853.6 jit_solution(12386188206055984860)
XLA Ops:
  10.5 8.9 %fusion.32 = f32[64,1,128,1]{2,1,3,0:T(1,128)S(1)} fusion(f32[64,4,128,1]{2,3,1,0:T(1,128)S(1)} %bitcast.345, bf16[64,4,128,128]{3,2,1,0:T(8,128)(2,1)} %param.11), kind=kOutput, calls=%fused_computation.141 | convolution fusion | flops 50331648 | bytes 8552448 | tf_op jit(solution)/shard_map/bsij,bsj->bi/dot_general | solution.py:30
  27.7 8.9 %fusion.33 = f32[64,1,128,1]{2,1,3,0:T(1,128)S(1)} fusion(f32[64,4,128,1]{2,3,1,0:T(1,128)S(1)} %bitcast.346, bf16[64,4,128,128]{3,2,1,0:T(8,128)(2,1)} %param.11), kind=kOutput, calls=%fused_computation.142 | convolution fusion | flops 50331648 | bytes 8552448 | tf_op jit(solution)/shard_map/bsij,bsj->bi/dot_general | solution.py:30
  45.1 8.9 %fusion.34 = f32[64,1,128,1]{2,1,3,0:T(1,128)S(1)} fusion(f32[64,4,128,1]{2,3,1,0:T(1,128)S(1)} %bitcast.347, bf16[64,4,128,128]{3,2,1,0:T(8,128)(2,1)} %param.11), kind=kOutput, calls=%fused_computation.143 | convolution fusion | flops 50331648 | bytes 8552448 | tf_op jit(solution)/shard_map/bsij,bsj->bi/dot_general | solution.py:30
  54.1 4.8 collective-permute-start.6
  62.7 8.9 %fusion.35 = f32[64,1,128,1]{2,1,3,0:T(1,128)S(1)} fusion(f32[64,4,128,1]{2,3,1,0:T(1,128)S(1)} %bitcast.348, bf16[64,4,128,128]{3,2,1,0:T(8,128)(2,1)} %param.11), kind=kOutput, calls=%fused_computation.144 | convolution fusion | flops 50331648 | bytes 8552448 | tf_op jit(solution)/shard_map/bsij,bsj->bi/dot_general | solution.py:30
  71.7 4.8 collective-permute-start.8
  80.3 8.9 %fusion.36 = f32[64,1,128,1]{2,1,3,0:T(1,128)S(1)} fusion(f32[64,4,128,1]{2,3,1,0:T(1,128)S(1)} %bitcast.349, bf16[64,4,128,128]{3,2,1,0:T(8,128)(2,1)} %param.11), kind=kOutput, calls=%fused_computation.145 | convolution fusion | flops 50331648 | bytes 8552448 | tf_op jit(solution)/shard_map/bsij,bsj->bi/dot_general | solution.py:30
  89.2 4.8 collective-permute-start.10
  97.9 8.9 %fusion.37 = f32[64,1,128,1]{2,1,3,0:T(1,128)S(1)} fusion(f32[64,4,128,1]{2,3,1,0:T(1,128)S(1)} %bitcast.350, bf16[64,4,128,128]{3,2,1,0:T(8,128)(2,1)} %param.11), kind=kOutput, calls=%fused_computation.146 | convolution fusion | flops 50331648 | bytes 8552448 | tf_op jit(solution)/shard_map/bsij,bsj->bi/dot_general | solution.py:30
  106.8 4.8 collective-permute-start.12
  115.4 8.9 %fusion.38 = f32[64,1,128,1]{2,1,3,0:T(1,128)S(1)} fusion(f32[64,4,128,1]{2,3,1,0:T(1,128)S(1)} %bitcast.351, bf16[64,4,128,128]{3,2,1,0:T(8,128)(2,1)} %param.11), kind=kOutput, calls=%fused_computation.147 | convolution fusion | flops 50331648 | bytes 8552448 | tf_op jit(solution)/shard_map/bsij,bsj->bi/dot_general | solution.py:30
  124.4 4.8 collective-permute-start.14
  133.0 8.9 %fusion.39 = f32[64,1,128,1]{2,1,3,0:T(1,128)S(1)} fusion(f32[64,4,128,1]{2,3,1,0:T(1,128)S(1)} %bitcast.352, bf16[64,4,128,128]{3,2,1,0:T(8,128)(2,1)} %param.11), kind=kOutput, calls=%fused_computation.148 | convolution fusion | flops 50331648 | bytes 8552448 | tf_op jit(solution)/shard_map/bsij,bsj->bi/dot_general | solution.py:30
  142.0 4.8 collective-permute-start.16
  150.6 8.9 %fusion.40 = f32[64,1,128,1]{2,1,3,0:T(1,128)S(1)} fusion(f32[64,4,128,1]{2,3,1,0:T(1,128)S(1)} %bitcast.353, bf16[64,4,128,128]{3,2,1,0:T(8,128)(2,1)} %param.11), kind=kOutput, calls=%fused_computation.149 | convolution fusion | flops 50331648 | bytes 8552448 | tf_op jit(solution)/shard_map/bsij,bsj->bi/dot_general | solution.py:30
  159.5 4.8 collective-permute-start.18
  168.2 8.9 %fusion.41 = f32[64,1,128,1]{2,1,3,0:T(1,128)S(1)} fusion(f32[64,4,128,1]{2,3,1,0:T(1,128)S(1)} %bitcast.354, bf16[64,4,128,128]{3,2,1,0:T(8,128)(2,1)} %param.11), kind=kOutput, calls=%fused_computation.150 | convolution fusion | flops 50331648 | bytes 8552448 | tf_op jit(solution)/shard_map/bsij,bsj->bi/dot_general | solution.py:30
  177.1 4.8 collective-permute-start.20
  185.8 8.9 %fusion.42 = f32[64,1,128,1]{2,1,3,0:T(1,128)S(1)} fusion(f32[64,4,128,1]{2,3,1,0:T(1,128)S(1)} %bitcast.355, bf16[64,4,128,128]{3,2,1,0:T(8,128)(2,1)} %param.11), kind=kOutput, calls=%fused_computation.151 | convolution fusion | flops 50331648 | bytes 8552448 | tf_op jit(solution)/shard_map/bsij,bsj->bi/dot_general | solution.py:30
  194.7 4.8 collective-permute-start.22
  203.3 8.9 %fusion.43 = f32[64,1,128,1]{2,1,3,0:T(1,128)S(1)} fusion(f32[64,4,128,1]{2,3,1,0:T(1,128)S(1)} %bitcast.356, bf16[64,4,128,128]{3,2,1,0:T(8,128)(2,1)} %param.11), kind=kOutput, calls=%fused_computation.152 | convolution fusion | flops 50331648 | bytes 8552448 | tf_op jit(solution)/shard_map/bsij,bsj->bi/dot_general | solution.py:30
  212.3 4.8 collective-permute-start.24
  220.9 8.9 %fusion.44 = f32[64,1,128,1]{2,1,3,0:T(1,128)S(1)} fusion(f32[64,4,128,1]{2,3,1,0:T(1,128)S(1)} %bitcast.357, bf16[64,4,128,128]{3,2,1,0:T(8,128)(2,1)} %param.11), kind=kOutput, calls=%fused_computation.153 | convolution fusion | flops 50331648 | bytes 8552448 | tf_op jit(solution)/shard_map/bsij,bsj->bi/dot_general | solution.py:30
  229.9 4.8 collective-permute-start.26
  238.5 8.9 %fusion.45 = f32[64,1,128,1]{2,1,3,0:T(1,128)S(1)} fusion(f32[64,4,128,1]{2,3,1,0:T(1,128)S(1)} %bitcast.358, bf16[64,4,128,128]{3,2,1,0:T(8,128)(2,1)} %param.11), kind=kOutput, calls=%fused_computation.154 | convolution fusion | flops 50331648 | bytes 8552448 | tf_op jit(solution)/shard_map/bsij,bsj->bi/dot_general | solution.py:30
  247.4 4.8 collective-permute-start.28
  256.1 8.9 %fusion.46 = f32[64,1,128,1]{2,1,3,0:T(1,128)S(1)} fusion(f32[64,4,128,1]{2,3,1,0:T(1,128)S(1)} %bitcast.359, bf16[64,4,128,128]{3,2,1,0:T(8,128)(2,1)} %param.11), kind=kOutput, calls=%fused_computation.155 | convolution fusion | flops 50331648 | bytes 8552448 | tf_op jit(solution)/shard_map/bsij,bsj->bi/dot_general | solution.py:30
  265.0 4.8 collective-permute-start.30
  273.6 8.9 %fusion.47 = f32[64,1,128,1]{2,1,3,0:T(1,128)S(1)} fusion(f32[64,4,128,1]{2,3,1,0:T(1,128)S(1)} %bitcast.360, bf16[64,4,128,128]{3,2,1,0:T(8,128)(2,1)} %param.11), kind=kOutput, calls=%fused_computation.156 | convolution fusion | flops 50331648 | bytes 8552448 | tf_op jit(solution)/shard_map/bsij,bsj->bi/dot_general | solution.py:30
  282.6 4.8 collective-permute-start.32
  291.2 8.9 %fusion.48 = f32[64,1,128,1]{2,1,3,0:T(1,128)S(1)} fusion(f32[64,4,128,1]{2,3,1,0:T(1,128)S(1)} %bitcast.361, bf16[64,4,128,128]{3,2,1,0:T(8,128)(2,1)} %param.11), kind=kOutput, calls=%fused_computation.157 | convolution fusion | flops 50331648 | bytes 8552448 | tf_op jit(solution)/shard_map/bsij,bsj->bi/dot_general | solution.py:30
  300.2 4.8 collective-permute-start.34
  308.8 8.9 %fusion.49 = f32[64,1,128,1]{2,1,3,0:T(1,128)S(1)} fusion(f32[64,4,128,1]{2,3,1,0:T(1,128)S(1)} %bitcast.362, bf16[64,4,128,128]{3,2,1,0:T(8,128)(2,1)} %param.11), kind=kOutput, calls=%fused_computation.158 | convolution fusion | flops 50331648 | bytes 8552448 | tf_op jit(solution)/shard_map/bsij,bsj->bi/dot_general | solution.py:30
  317.7 4.8 collective-permute-start.36
  326.4 8.9 %fusion.50 = f32[64,1,128,1]{2,1,3,0:T(1,128)S(1)} fusion(f32[64,4,128,1]{2,3,1,0:T(1,128)S(1)} %bitcast.363, bf16[64,4,128,128]{3,2,1,0:T(8,128)(2,1)} %param.11), kind=kOutput, calls=%fused_computation.159 | convolution fusion | flops 50331648 | bytes 8552448 | tf_op jit(solution)/shard_map/bsij,bsj->bi/dot_general | solution.py:30
  335.3 4.8 collective-permute-start.38
  344.0 8.9 %fusion.51 = f32[64,1,128,1]{2,1,3,0:T(1,128)S(1)} fusion(f32[64,4,128,1]{2,3,1,0:T(1,128)S(1)} %bitcast.364, bf16[64,4,128,128]{3,2,1,0:T(8,128)(2,1)} %param.11), kind=kOutput, calls=%fused_computation.160 | convolution fusion | flops 50331648 | bytes 8552448 | tf_op jit(solution)/shard_map/bsij,bsj->bi/dot_general | solution.py:30
  352.9 4.8 collective-permute-start.40
  361.5 8.9 %fusion.52 = f32[64,1,128,1]{2,1,3,0:T(1,128)S(1)} fusion(f32[64,4,128,1]{2,3,1,0:T(1,128)S(1)} %bitcast.365, bf16[64,4,128,128]{3,2,1,0:T(8,128)(2,1)} %param.11), kind=kOutput, calls=%fused_computation.161 | convolution fusion | flops 50331648 | bytes 8552448 | tf_op jit(solution)/shard_map/bsij,bsj->bi/dot_general | solution.py:30
  370.5 4.8 collective-permute-start.42
  379.1 8.9 %fusion.53 = f32[64,1,128,1]{2,1,3,0:T(1,128)S(1)} fusion(f32[64,4,128,1]{2,3,1,0:T(1,128)S(1)} %bitcast.366, bf16[64,4,128,128]{3,2,1,0:T(8,128)(2,1)} %param.11), kind=kOutput, calls=%fused_computation.162 | convolution fusion | flops 50331648 | bytes 8552448 | tf_op jit(solution)/shard_map/bsij,bsj->bi/dot_general | solution.py:30
  388.0 4.8 collective-permute-start.44
  396.7 8.9 %fusion.54 = f32[64,1,128,1]{2,1,3,0:T(1,128)S(1)} fusion(f32[64,4,128,1]{2,3,1,0:T(1,128)S(1)} %bitcast.367, bf16[64,4,128,128]{3,2,1,0:T(8,128)(2,1)} %param.11), kind=kOutput, calls=%fused_computation.163 | convolution fusion | flops 50331648 | bytes 8552448 | tf_op jit(solution)/shard_map/bsij,bsj->bi/dot_general | solution.py:30
  405.6 4.8 collective-permute-start.46
  414.3 8.9 %fusion.55 = f32[64,1,128,1]{2,1,3,0:T(1,128)S(1)} fusion(f32[64,4,128,1]{2,3,1,0:T(1,128)S(1)} %bitcast.368, bf16[64,4,128,128]{3,2,1,0:T(8,128)(2,1)} %param.11), kind=kOutput, calls=%fused_computation.164 | convolution fusion | flops 50331648 | bytes 8552448 | tf_op jit(solution)/shard_map/bsij,bsj->bi/dot_general | solution.py:30
  423.2 4.8 collective-permute-start.48
  431.8 8.9 %fusion.56 = f32[64,1,128,1]{2,1,3,0:T(1,128)S(1)} fusion(f32[64,4,128,1]{2,3,1,0:T(1,128)S(1)} %bitcast.369, bf16[64,4,128,128]{3,2,1,0:T(8,128)(2,1)} %param.11), kind=kOutput, calls=%fused_computation.165 | convolution fusion | flops 50331648 | bytes 8552448 | tf_op jit(solution)/shard_map/bsij,bsj->bi/dot_general | solution.py:30
  440.8 4.8 collective-permute-start.50
  449.4 8.9 %fusion.57 = f32[64,1,128,1]{2,1,3,0:T(1,128)S(1)} fusion(f32[64,4,128,1]{2,3,1,0:T(1,128)S(1)} %bitcast.370, bf16[64,4,128,128]{3,2,1,0:T(8,128)(2,1)} %param.11), kind=kOutput, calls=%fused_computation.166 | convolution fusion | flops 50331648 | bytes 8552448 | tf_op jit(solution)/shard_map/bsij,bsj->bi/dot_general | solution.py:30
  458.4 4.8 collective-permute-start.52
  467.0 8.9 %fusion.58 = f32[64,1,128,1]{2,1,3,0:T(1,128)S(1)} fusion(f32[64,4,128,1]{2,3,1,0:T(1,128)S(1)} %bitcast.371, bf16[64,4,128,128]{3,2,1,0:T(8,128)(2,1)} %param.11), kind=kOutput, calls=%fused_computation.167 | convolution fusion | flops 50331648 | bytes 8552448 | tf_op jit(solution)/shard_map/bsij,bsj->bi/dot_general | solution.py:30
  475.9 4.8 collective-permute-start.54
  484.6 8.9 %fusion.59 = f32[64,1,128,1]{2,1,3,0:T(1,128)S(1)} fusion(f32[64,4,128,1]{2,3,1,0:T(1,128)S(1)} %bitcast.372, bf16[64,4,128,128]{3,2,1,0:T(8,128)(2,1)} %param.11), kind=kOutput, calls=%fused_computation.168 | convolution fusion | flops 50331648 | bytes 8552448 | tf_op jit(solution)/shard_map/bsij,bsj->bi/dot_general | solution.py:30
  493.5 4.8 collective-permute-start.56
  502.1 8.9 %fusion.60 = f32[64,1,128,1]{2,1,3,0:T(1,128)S(1)} fusion(f32[64,4,128,1]{2,3,1,0:T(1,128)S(1)} %bitcast.373, bf16[64,4,128,128]{3,2,1,0:T(8,128)(2,1)} %param.11), kind=kOutput, calls=%fused_computation.169 | convolution fusion | flops 50331648 | bytes 8552448 | tf_op jit(solution)/shard_map/bsij,bsj->bi/dot_general | solution.py:30
  511.1 4.8 collective-permute-start.58
  519.7 8.9 %fusion.61 = f32[64,1,128,1]{2,1,3,0:T(1,128)S(1)} fusion(f32[64,4,128,1]{2,3,1,0:T(1,128)S(1)} %bitcast.374, bf16[64,4,128,128]{3,2,1,0:T(8,128)(2,1)} %param.11), kind=kOutput, calls=%fused_computation.170 | convolution fusion | flops 50331648 | bytes 8552448 | tf_op jit(solution)/shard_map/bsij,bsj->bi/dot_general | solution.py:30
  528.7 4.8 collective-permute-start.60
  537.3 8.9 %fusion.62 = f32[64,1,128,1]{2,1,3,0:T(1,128)S(1)} fusion(f32[64,4,128,1]{2,3,1,0:T(1,128)S(1)} %bitcast.375, bf16[64,4,128,128]{3,2,1,0:T(8,128)(2,1)} %param.11), kind=kOutput, calls=%fused_computation.171 | convolution fusion | flops 50331648 | bytes 8552448 | tf_op jit(solution)/shard_map/bsij,bsj->bi/dot_general | solution.py:30
  554.9 8.9 %fusion.63 = f32[64,1,128,1]{2,1,3,0:T(1,128)S(1)} fusion(f32[64,4,128,1]{2,3,1,0:T(1,128)S(1)} %bitcast.344, bf16[64,4,128,128]{3,2,1,0:T(8,128)(2,1)} %param.11), kind=kOutput, calls=%fused_computation.172 | convolution fusion | flops 50331648 | bytes 8552448 | tf_op jit(solution)/shard_map/bsij,bsj->bi/dot_general | solution.py:30
  564.6 8.4 all-to-all-start
  573.1 7.9 all-to-all-done
  581.2 135.5 %gather_fusion.33 = f32[24576]{0:T(1024)S(1)} fusion(f32[8192]{0:T(1024)S(1)} %bitcast.340, s32[24576]{0:T(1024)S(1)} %broadcast_clamp_fusion), kind=kCustom, calls=%fused_computation.33 | custom fusion | bytes 294912 | tf_op jit(solution)/shard_map/gather | solution.py:25
  716.7 135.5 %gather_fusion.32 = f32[24576]{0:T(1024)S(1)} fusion(f32[8192]{0:T(1024)S(1)} %bitcast.339, s32[24576]{0:T(1024)S(1)} %broadcast_clamp_fusion), kind=kCustom, calls=%fused_computation.32 | custom fusion | bytes 294912 | tf_op jit(solution)/shard_map/gather | solution.py:25
  (254 shorter events, 144.2 us)
Async XLA Ops:
  1.4 4.6 collective-permute-start
  3.8 5.2 collective-permute-start.1
  19.5 5.7 collective-permute-start.2
  23.9 3.1 collective-permute-start.3
  36.6 6.0 collective-permute-start.4
  41.3 3.1 collective-permute-start.5
  54.1 6.1 collective-permute-start.6
  58.9 3.1 collective-permute-start.7
  71.7 6.1 collective-permute-start.8
  76.5 3.1 collective-permute-start.9
  89.2 6.3 collective-permute-start.10
  94.1 3.1 collective-permute-start.11
  106.8 6.1 collective-permute-start.12
  111.6 3.1 collective-permute-start.13
  124.4 6.1 collective-permute-start.14
  129.2 3.1 collective-permute-start.15
  142.0 6.1 collective-permute-start.16
  146.8 3.1 collective-permute-start.17
  159.5 6.1 collective-permute-start.18
  164.4 3.1 collective-permute-start.19
  177.1 6.3 collective-permute-start.20
  181.9 3.1 collective-permute-start.21
  194.7 6.1 collective-permute-start.22
  199.5 3.1 collective-permute-start.23
  212.3 6.1 collective-permute-start.24
  217.1 3.1 collective-permute-start.25
  229.9 6.1 collective-permute-start.26
  234.7 3.1 collective-permute-start.27
  247.4 6.1 collective-permute-start.28
  252.3 3.1 collective-permute-start.29
  265.0 6.5 collective-permute-start.30
  269.8 3.1 collective-permute-start.31
  282.6 6.1 collective-permute-start.32
  287.4 3.1 collective-permute-start.33
  300.2 6.1 collective-permute-start.34
  305.0 3.1 collective-permute-start.35
  317.7 6.1 collective-permute-start.36
  322.6 3.1 collective-permute-start.37
  335.3 6.1 collective-permute-start.38
  340.1 3.1 collective-permute-start.39
  352.9 6.3 collective-permute-start.40
  357.7 3.1 collective-permute-start.41
  370.5 6.1 collective-permute-start.42
  375.3 3.1 collective-permute-start.43
  388.0 6.1 collective-permute-start.44
  392.9 3.1 collective-permute-start.45
  405.6 6.1 collective-permute-start.46
  410.4 3.1 collective-permute-start.47
  423.2 6.1 collective-permute-start.48
  428.0 3.1 collective-permute-start.49
  440.8 6.3 collective-permute-start.50
  445.6 3.1 collective-permute-start.51
  458.4 6.1 collective-permute-start.52
  463.2 3.1 collective-permute-start.53
  475.9 6.1 collective-permute-start.54
  480.8 3.1 collective-permute-start.55
  493.5 6.1 collective-permute-start.56
  498.3 3.1 collective-permute-start.57
  511.1 6.1 collective-permute-start.58
  515.9 3.1 collective-permute-start.59
  528.7 6.4 collective-permute-start.60
  546.3 6.3 collective-permute-start.62
  551.1 3.1 collective-permute-start.63
  564.6 16.4 %all-to-all-start = ((f32[4,16,512]{2,0,1:T(4,128)}), f32[4,16,512]{2,0,1:T(4,128)S(1)}, u32[]{:S(2)}, u32[]{:S(2)}) async-start(f32[4,16,512]{2,0,1:T(4,128)} %pad_maximum_fusion), calls=%async_computation | async-start | bytes 262144 | tf_op jit(solution)/shard_map/all_to_all | solution.py:54
  (7 other events, 246.5 us)
where the time goes:
time: 863 us; the launch traced here: 854 us
  local copies, waits for them, and re-layouts  296 us (34%)
  matrix products  285 us (33%)
  starting transfers between devices  202 us (23%)
  waiting for transfers between devices  64.2 us (7%)
    dot_general x32, matrix products, couple(): jnp.einsum('bsij,bsj->bi', blocks, nearby, precision=lax.Precision.HIGHES...  285 us
    gather x4, local copies, waits for them, and re-layouts, interpolate(): sampled = flattened[grid_nodes]  271 us
    ppermute x32, starting transfers between devices, padded_2(): lax.ppermute(lax.slice_in_dim(block, block.shape[dim] - width, None, axis...  151 us
    ppermute x32, waiting for transfers between devices, padded_2(): lax.ppermute(lax.slice_in_dim(block, 0, width, axis=dim), axis, backward)  56.2 us
    ppermute x32, starting transfers between devices, padded_2(): lax.ppermute(lax.slice_in_dim(block, 0, width, axis=dim), axis, backward)  42.8 us
    gather x32, local copies, waits for them, and re-layouts, local(): coupled = couple(coupling, padded[neighbours])  23.3 us
  transfers between devices with their start and end apart: 65, of which 33 were waited for; matrix products, arithmetic and copies ran while one was open for 0% of the time, Pallas kernels for 0%

commit v1 on v0

v1 whole, which is shorter than its diff:
```python
import functools

import jax
import jax.numpy as jnp
from jax import lax
from jax.experimental import pallas as pl
from jax.experimental.pallas import tpu as pltpu
from jax.sharding import PartitionSpec as P

SWEEPS = 8
MESH = pl.DeviceIdType.MESH
F32, BF16 = jnp.float32, jnp.bfloat16


def surge_kernel(
    domains,
    eta_ref, forcing_ref, diag_ref, nb_ref, wet_ref, coupling_ref,
    out_ref,
    raw, weights, padded, onehot, surface, source, scale, highest, partial, sending, landing,
    load_sem, send_sem, recv_sem, strip_send, strip_recv,
):
    steps, rows, node = forcing_ref.shape
    slots = coupling_ref.shape[1]
    margin = rows // 2
    share = rows // domains
    chunk = 8
    me = lax.axis_index("dom")
    has_left, has_right = me > 0, me < domains - 1

    loads = [
        pltpu.make_async_copy(
            coupling_ref.at[pl.ds(c * chunk, chunk)], raw.at[pl.ds(c * chunk, chunk)], load_sem.at[c]
        )
        for c in range(rows // chunk)
    ]
    for load in loads:
        load.start()

    padded[...] = jnp.zeros_like(padded)
    barrier = pltpu.get_barrier_semaphore()

    def greet(k, carry):
        peer = lax.rem(me + k, domains)
        pl.semaphore_signal(barrier, inc=1, device_id={"dom": peer}, device_id_type=MESH)
        return carry

    lax.fori_loop(1, domains, greet, 0)

    scale[...] = wet_ref[...].astype(F32) / diag_ref[...]
    lane = lax.broadcasted_iota(jnp.int32, (rows, 2 * rows), 1)
    for s in range(1, slots):
        onehot[(s - 1) * rows : s * rows, :] = (nb_ref[:, s : s + 1] == lane).astype(F32).astype(BF16)

    def split(value):
        high = value.astype(BF16).astype(F32)
        return high, value - high

    def store(slot, row, count):
        high, low = split(surface[row : row + count, :])
        padded[slot, margin + row : margin + row + count, :node] = high.astype(BF16)
        padded[slot, margin + row : margin + row + count, node:] = low.astype(BF16)

    def exchange(slot, side):
        return pltpu.make_async_remote_copy(
            src_ref=padded.at[slot, pl.ds(margin + side * margin, margin)],
            dst_ref=padded.at[slot, pl.ds(margin + rows if side == 0 else 0, margin)],
            send_sem=send_sem.at[slot, side],
            recv_sem=recv_sem.at[slot, side],
            device_id={"dom": me - 1 if side == 0 else me + 1},
            device_id_type=MESH,
        )

    def arrival(slot, side):
        return pltpu.make_async_remote_copy(
            src_ref=padded.at[slot, pl.ds(margin + side * margin, margin)],
            dst_ref=padded.at[slot, pl.ds(margin + rows if side == 0 else 0, margin)],
            send_sem=send_sem.at[slot, side],
            recv_sem=recv_sem.at[slot, side],
            device_id={"dom": me + 1 if side == 0 else me - 1},
            device_id_type=MESH,
        )

    def send(slot, side, condition):
        @pl.when(jnp.logical_and(has_left if side == 0 else has_right, condition))
        def _():
            exchange(slot, side).start()

    surface[...] = eta_ref[...]
    source[...] = diag_ref[...] * eta_ref[...] + forcing_ref[0]
    highest[...] = jnp.full((rows, node), -jnp.inf, F32)
    store(0, 0, rows)

    pl.semaphore_wait(barrier, domains - 1)
    send(0, 0, True)
    send(0, 1, True)

    for c, load in enumerate(loads):
        load.wait()

        def arrange(pair, carry):
            for half in range(2):
                for s in range(slots):
                    weights[pair, s * node : (s + 1) * node, half * node : (half + 1) * node] = raw[
                        2 * pair + half, s
                    ].T
            return carry

        lax.fori_loop(c * chunk // 2, (c + 1) * chunk // 2, arrange, 0)

    sub = lax.broadcasted_iota(jnp.int32, (8, node), 0)

    def products(group, left, first, last):
        result = jnp.zeros((8, node), F32)
        for q in range(4):
            pair = group * 4 + q
            both = jnp.dot(
                left, weights[pair, first * node : last * node, :], preferred_element_type=F32
            )
            both = both[:8] + both[8:]
            result = jnp.where(sub == 2 * q, both[:, :node], result)
            result = jnp.where(sub == 2 * q + 1, both[:, node:], result)
        return result

    def sweep(slot, more):
        for group in range(rows // 8):
            at = slice(group * 8, group * 8 + 8)
            left = jnp.concatenate(split(surface[at, :]), axis=0).astype(BF16)
            partial[at, :] = products(group, left, 0, 1)

        @pl.when(has_right)
        def _():
            arrival(slot, 0).wait_recv()
            exchange(slot, 1).wait_send()

        @pl.when(has_left)
        def _():
            arrival(slot, 1).wait_recv()
            exchange(slot, 0).wait_send()

        near = jnp.dot(onehot[...], padded[slot], preferred_element_type=F32)
        for group in range(rows // 8):
            at = slice(group * 8, group * 8 + 8)
            left = jnp.concatenate(
                [
                    jnp.concatenate(
                        [
                            near[s * rows + group * 8 : s * rows + group * 8 + 8, :node],
                            near[s * rows + group * 8 : s * rows + group * 8 + 8, node:],
                        ],
                        axis=0,
                    )
                    for s in range(slots - 1)
                ],
                axis=1,
            ).astype(BF16)
            coupled = partial[at, :] + products(group, left, 1, slots)
            surface[at, :] = (source[at, :] - coupled) * scale[at, :]
            if group % 2 == 1:
                store(1 - slot, group * 8 - 8, 16)
            if group == rows // 16 - 1:
                send(1 - slot, 0, more)
            if group == rows // 8 - 1:
                send(1 - slot, 1, more)

    def step(t, carry):
        def two(j, carry):
            sweep(0, True)
            sweep(1, jnp.logical_or(t < steps - 1, j < SWEEPS // 2 - 1))
            return carry

        lax.fori_loop(0, SWEEPS // 2, two, 0)
        after = lax.rem(t + 1, steps)
        highest[...] = jnp.maximum(highest[...], surface[...])
        source[...] = diag_ref[...] * surface[...] + forcing_ref[after]
        return carry

    lax.fori_loop(0, steps, step, 0)

    for q in range(domains):
        sending[q, :share, :] = highest[q * share : (q + 1) * share, :]
        sending[q, share:, :] = surface[q * share : (q + 1) * share, :]

    def strip(to, by):
        return pltpu.make_async_remote_copy(
            src_ref=sending.at[to],
            dst_ref=landing.at[by],
            send_sem=strip_send.at[to],
            recv_sem=strip_recv.at[by],
            device_id={"dom": to},
            device_id_type=MESH,
        )

    def start(k, carry):
        strip(lax.rem(me + k, domains), me).start()
        return carry

    lax.fori_loop(1, domains, start, 0)
    landing[me] = sending[me]

    def finish(k, carry):
        peer = lax.rem(me + k, domains)
        strip(peer, peer).wait_recv()
        strip(peer, me).wait_send()
        return carry

    lax.fori_loop(1, domains, finish, 0)
    for q in range(domains):
        out_ref[0, q * share : (q + 1) * share, :] = landing[q, :share, :]
        out_ref[1, q * share : (q + 1) * share, :] = landing[q, share:, :]


def grid_kernel(table_ref, nodes_ref, weights_ref, level_ref, final_ref):
    rows, node = table_ref.shape[1:]

    def cells(c, carry):
        at = pl.ds(pl.multiple_of(c * 8, 8), 8)
        totals = [jnp.zeros((8, node), F32)] * 2
        for k in range(nodes_ref.shape[0]):
            index = nodes_ref[k, at, :]
            row, lane = index // node, index % node
            found = [jnp.zeros((8, node), F32)] * 2
            for r in range(rows):
                hit = row == r
                for f in range(2):
                    picked = jnp.take_along_axis(
                        jnp.broadcast_to(table_ref[f, r : r + 1, :], (8, node)), lane, axis=1
                    )
                    found[f] = jnp.where(hit, picked, found[f])
            weight = weights_ref[k, at, :]
            totals = [total + weight * value for total, value in zip(totals, found)]
        level_ref[at, :] = totals[0]
        final_ref[at, :] = totals[1]
        return carry

    lax.fori_loop(0, nodes_ref.shape[1] // 8, cells, 0)


def local(domains, eta_start, forcing, diagonal, coupling, neighbours, wet, grid_nodes, grid_weights):
    steps, rows, node = forcing.shape
    slots = coupling.shape[1]
    share = rows // domains
    vmem = pl.BlockSpec(memory_space=pltpu.VMEM)
    fields = pl.pallas_call(
        functools.partial(surge_kernel, domains),
        out_shape=jax.ShapeDtypeStruct((2, rows, node), F32),
        in_specs=[vmem] * 5 + [pl.BlockSpec(memory_space=pl.ANY)],
        out_specs=vmem,
        scratch_shapes=[
            pltpu.VMEM(coupling.shape, BF16),
            pltpu.VMEM((rows // 2, slots * node, 2 * node), BF16),
            pltpu.VMEM((2, 2 * rows, 2 * node), BF16),
            pltpu.VMEM(((slots - 1) * rows, 2 * rows), BF16),
            pltpu.VMEM((rows, node), F32),
            pltpu.VMEM((rows, node), F32),
            pltpu.VMEM((rows, node), F32),
            pltpu.VMEM((rows, node), F32),
            pltpu.VMEM((rows, node), F32),
            pltpu.VMEM((domains, 2 * share, node), F32),
            pltpu.VMEM((domains, 2 * share, node), F32),
            pltpu.SemaphoreType.DMA((rows // 8,)),
            pltpu.SemaphoreType.DMA((2, 2)),
            pltpu.SemaphoreType.DMA((2, 2)),
            pltpu.SemaphoreType.DMA((domains,)),
            pltpu.SemaphoreType.DMA((domains,)),
        ],
        compiler_params=pltpu.CompilerParams(
            collective_id=0, has_side_effects=True, vmem_limit_bytes=40 << 20
        ),
    )(eta_start, forcing, diagonal, neighbours, wet, coupling)
    cells = grid_nodes.shape[1]
    shaped = (grid_nodes.shape[0], cells // node, node)
    level, final = pl.pallas_call(
        grid_kernel,
        out_shape=[jax.ShapeDtypeStruct((cells // node, node), F32)] * 2,
        in_specs=[vmem] * 3,
        out_specs=[vmem] * 2,
    )(fields, grid_nodes.reshape(shaped), grid_weights.reshape(shaped))
    return level.reshape(-1), final.reshape(-1)


def solution(mesh):
    in_specs = (
        P(("storm", "dom"), None),
        P(None, ("storm", "dom"), None),
        P("dom", None),
        P("dom", None, None, None),
        P("dom", None),
        P("dom", None),
        P(None, "dom"),
        P(None, "dom"),
    )
    out_specs = (P(("storm", "dom")), P(("storm", "dom")))
    return jax.shard_map(
        functools.partial(local, mesh.shape["dom"]),
        mesh=mesh, in_specs=in_specs, out_specs=out_specs, check_vma=False,
    )
```

time: 863 us -> 145 us (0.17)
  local copies, waits for them, and re-layouts: 296 us -> 9.22 us
  matrix products: 285 us -> 0 us
  starting transfers between devices: 202 us -> 0 us
  Pallas kernels: 0 us -> 134 us
  waiting for transfers between devices: 64.2 us -> 0 us
    gather x36 -> x0, local copies, waits for them, and re-layouts: 295 us -> none  [the longest x4 271 us: interpolate(): sampled = flattened[grid_nodes]]
    dot_general x32 -> x0, matrix products: 285 us -> none  [couple(): jnp.einsum('bsij,bsj->bi', blocks, nearby, precision=lax.Precision.HIGHES...]
    ppermute x64 -> x0, starting transfers between devices: 194 us -> none  [the longest x32 151 us: padded_2(): lax.ppermute(lax.slice_in_dim(block, block.shape[dim] - width, None, axis...]
    pallas_call x0 -> x2, Pallas kernels: none -> 134 us  [the longest x1 129 us: local(): pl.pallas_call(functools.partial(surge_kernel, domains), out_shape=jax.Sh...]
    ppermute x64 -> x0, waiting for transfers between devices: 56.3 us -> none  [the longest x32 56.2 us: padded_2(): lax.ppermute(lax.slice_in_dim(block, 0, width, axis=dim), axis, backward)]
    unnamed x13 -> x19, local copies, waits for them, and re-layouts: 0.05 us -> 9.22 us
  transfers between devices with their start and end apart: 65 -> 0, of which waited for: 33 -> 0; matrix products, arithmetic and copies ran while one was open for 0% -> 0% of each run, Pallas kernels for 0% -> 0%
where the time goes in v1:
time: 145 us; the launch traced here: 144 us
  Pallas kernels  134 us (92%)
  local copies, waits for them, and re-layouts  9.22 us (6%)
    pallas_call x1, Pallas kernels, local(): pl.pallas_call(functools.partial(surge_kernel, domains), out_shape=jax.Sh...  129 us
    unnamed x19, local copies, waits for them, and re-layouts  9.22 us
    pallas_call x1, Pallas kernels, local(): pl.pallas_call(grid_kernel, out_shape=[jax.ShapeDtypeStruct((cells // nod...  5.54 us

profile of v1, /device:TPU:0, one launch (start us, length us, event | category | flops | bytes accessed | tf_op | source)
XLA Modules:
  0.0 144.2 jit_solution(15104399848482142853)
XLA Ops:
  0.6 0.8 copy.10.nb_ref
  1.4 0.0 copy-start
  1.4 3.4 %copy-done = bf16[64,4,128,128]{3,2,1,0:T(8,128)(2,1)S(1)} copy-done((bf16[64,4,128,128]{3,2,1,0:T(8,128)(2,1)S(1)}, bf16[64,4,128,128]{3,2,1,0:T(8,128)(2,1)}, u32[]{:S(2)}) %copy-start) | copy-done | bytes 8388632
  4.8 0.0 copy-start.2
  4.8 0.9 copy-done.2
  5.7 0.0 copy-start.3
  5.7 0.8 copy-done.3
  6.4 0.0 copy-start.4
  6.4 0.8 copy-done.4
  7.2 0.0 copy-start.5
  7.2 0.8 copy-done.5
  8.0 0.0 copy-start.6
  8.0 0.0 copy-start.7
  8.0 128.8 %shard_map.95.table_ref = f32[2,64,128]{2,1,0:T(8,128)S(1)} custom-call(f32[64,128]{1,0:T(8,128)S(1)} %copy-done.3, f32[4,64,128]{2,1,0:T(8,128)S(1)} %copy-done.2, f32[64,128]{1,0:T(8,128)S(1)} %copy-done.4, s32[64,4]{1,0:T(8,128)S(1)} %copy.10.nb_ref, s32[64,128]{1,0:T(8,128)S(1)} %copy-done.5, bf16[64,4,128,128]{3,2,1,0:T(8,128)(2,1)S(1)} %copy-done), custom_call_target="tpu_custom_call" | custom-call | tf_op jit(solution)/shard_map/pallas_call | solution.py:243
  136.8 0.0 copy-start.1
  136.8 0.6 copy-done.1
  137.4 0.0 copy-done.6
  137.4 0.6 copy.16
  138.0 0.0 copy-done.7
  138.0 0.6 copy.15
  138.7 5.5 %shard_map.96 = (f32[64,128]{1,0:T(8,128)}, f32[64,128]{1,0:T(8,128)}) custom-call(f32[2,64,128]{2,1,0:T(8,128)} %copy-done.1, s32[3,64,128]{2,1,0:T(8,128)} %bitcast.10, f32[3,64,128]{2,1,0:T(8,128)} %bitcast.11), custom_call_target="tpu_custom_call" | custom-call | tf_op jit(solution)/shard_map/pallas_call | solution.py:272
Async XLA Ops:
  1.4 3.4 %copy-start = (bf16[64,4,128,128]{3,2,1,0:T(8,128)(2,1)S(1)}, bf16[64,4,128,128]{3,2,1,0:T(8,128)(2,1)}, u32[]{:S(2)}) copy-start(bf16[64,4,128,128]{3,2,1,0:T(8,128)(2,1)} %coupling_ref.1) | copy-start | bytes 25165828
  4.8 0.9 copy-start.2
  5.7 0.8 copy-start.3
  6.4 0.8 copy-start.4
  7.2 0.8 copy-start.5
  8.0 129.4 %copy-start.6 = (s32[3,8192]{1,0:T(4,128)S(1)}, s32[3,8192]{1,0:T(4,128)}, u32[]{:S(2)}) copy-start(s32[3,8192]{1,0:T(4,128)} %param.14) | copy-start | bytes 294916
  8.0 130.1 %copy-start.7 = (f32[3,8192]{1,0:T(4,128)S(1)}, f32[3,8192]{1,0:T(4,128)}, u32[]{:S(2)}) copy-start(f32[3,8192]{1,0:T(4,128)} %param.15) | copy-start | bytes 294916
  136.8 0.6 copy-start.1

commit v2 on v1

--- a/solution.py
+++ b/solution.py
@@ -14,10 +14,10 @@
 
 def surge_kernel(
     domains,
-    eta_ref, forcing_ref, diag_ref, nb_ref, wet_ref, coupling_ref,
+    eta_hbm, forcing_hbm, diag_hbm, nb_hbm, wet_hbm, coupling_ref,
     out_ref,
-    raw, weights, padded, onehot, surface, source, scale, highest, partial, sending, landing,
-    load_sem, send_sem, recv_sem, strip_send, strip_recv,
+    eta_ref, forcing_ref, diag_ref, nb_ref, wet_ref, raw, weights, padded, onehot, nearby, surface, source, scale, highest, partial, sending, landing,
+    small_sem, load_sem, send_sem, recv_sem, strip_send, strip_recv,
 ):
     steps, rows, node = forcing_ref.shape
     slots = coupling_ref.shape[1]
@@ -25,7 +25,17 @@
     share = rows // domains
     chunk = 8
     me = lax.axis_index("dom")
-    has_left, has_right = me > 0, me < domains - 1
+    outer = lax.rem(me, 2)
+    inner = 1 - outer
+
+    small = [
+        pltpu.make_async_copy(source_ref, target_ref, small_sem.at[i])
+        for i, (source_ref, target_ref) in enumerate(
+            [(eta_hbm, eta_ref), (diag_hbm, diag_ref), (forcing_hbm, forcing_ref), (nb_hbm, nb_ref), (wet_hbm, wet_ref)]
+        )
+    ]
+    for load in small:
+        load.start()
 
     loads = [
         pltpu.make_async_copy(
@@ -46,6 +56,8 @@
 
     lax.fori_loop(1, domains, greet, 0)
 
+    for load in small:
+        load.wait()
     scale[...] = wet_ref[...].astype(F32) / diag_ref[...]
     lane = lax.broadcasted_iota(jnp.int32, (rows, 2 * rows), 1)
     for s in range(1, slots):
@@ -56,34 +68,34 @@
         return high, value - high
 
     def store(slot, row, count):
-        high, low = split(surface[row : row + count, :])
-        padded[slot, margin + row : margin + row + count, :node] = high.astype(BF16)
-        padded[slot, margin + row : margin + row + count, node:] = low.astype(BF16)
-
-    def exchange(slot, side):
+        high, low = split(surface[pl.ds(row, count), :])
+        padded[slot, pl.ds(margin + row, count), :node] = high.astype(BF16)
+        padded[slot, pl.ds(margin + row, count), node:] = low.astype(BF16)
+
+    def exchange(slot, side, step):
         return pltpu.make_async_remote_copy(
-            src_ref=padded.at[slot, pl.ds(margin + side * margin, margin)],
-            dst_ref=padded.at[slot, pl.ds(margin + rows if side == 0 else 0, margin)],
+            src_ref=padded.at[slot, pl.ds(pl.multiple_of(margin + side * margin, margin), margin)],
+            dst_ref=padded.at[slot, pl.ds(pl.multiple_of((1 - side) * (margin + rows), margin), margin)],
             send_sem=send_sem.at[slot, side],
             recv_sem=recv_sem.at[slot, side],
-            device_id={"dom": me - 1 if side == 0 else me + 1},
+            device_id={"dom": me + step * (2 * side - 1)},
             device_id_type=MESH,
         )
 
-    def arrival(slot, side):
-        return pltpu.make_async_remote_copy(
-            src_ref=padded.at[slot, pl.ds(margin + side * margin, margin)],
-            dst_ref=padded.at[slot, pl.ds(margin + rows if side == 0 else 0, margin)],
-            send_sem=send_sem.at[slot, side],
-            recv_sem=recv_sem.at[slot, side],
-            device_id={"dom": me + 1 if side == 0 else me - 1},
-            device_id_type=MESH,
-        )
+    def present(side):
+        peer = me + 2 * side - 1
+        return jnp.logical_and(peer >= 0, peer < domains)
 
     def send(slot, side, condition):
-        @pl.when(jnp.logical_and(has_left if side == 0 else has_right, condition))
+        @pl.when(jnp.logical_and(present(side), condition))
         def _():
-            exchange(slot, side).start()
+            exchange(slot, side, 1).start()
+
+    def receive(slot, side):
+        @pl.when(present(side))
+        def _():
+            exchange(slot, 1 - side, -1).wait_recv()
+            exchange(slot, side, 1).wait_send()
 
     surface[...] = eta_ref[...]
     source[...] = diag_ref[...] * eta_ref[...] + forcing_ref[0]
@@ -91,8 +103,8 @@
     store(0, 0, rows)
 
     pl.semaphore_wait(barrier, domains - 1)
-    send(0, 0, True)
-    send(0, 1, True)
+    send(0, outer, True)
+    send(0, inner, True)
 
     for c, load in enumerate(loads):
         load.wait()
@@ -109,10 +121,10 @@
 
     sub = lax.broadcasted_iota(jnp.int32, (8, node), 0)
 
-    def products(group, left, first, last):
+    def products(first_pair, left, first, last):
         result = jnp.zeros((8, node), F32)
         for q in range(4):
-            pair = group * 4 + q
+            pair = first_pair + q
             both = jnp.dot(
                 left, weights[pair, first * node : last * node, :], preferred_element_type=F32
             )
@@ -125,42 +137,32 @@
         for group in range(rows // 8):
             at = slice(group * 8, group * 8 + 8)
             left = jnp.concatenate(split(surface[at, :]), axis=0).astype(BF16)
-            partial[at, :] = products(group, left, 0, 1)
-
-        @pl.when(has_right)
-        def _():
-            arrival(slot, 0).wait_recv()
-            exchange(slot, 1).wait_send()
-
-        @pl.when(has_left)
-        def _():
-            arrival(slot, 1).wait_recv()
-            exchange(slot, 0).wait_send()
-
+            partial[at, :] = products(group * 4, left, 0, 1)
+
+        receive(slot, inner)
+        receive(slot, outer)
         near = jnp.dot(onehot[...], padded[slot], preferred_element_type=F32)
-        for group in range(rows // 8):
-            at = slice(group * 8, group * 8 + 8)
+        for s in range(slots - 1):
+            nearby[s] = near[s * rows : (s + 1) * rows, :]
+        count = rows // 8
+        for turn in range(count):
+            group = turn + (outer if turn < count // 2 else -outer) * (count // 2)
+            at = pl.ds(pl.multiple_of(group * 8, 8), 8)
             left = jnp.concatenate(
                 [
-                    jnp.concatenate(
-                        [
-                            near[s * rows + group * 8 : s * rows + group * 8 + 8, :node],
-                            near[s * rows + group * 8 : s * rows + group * 8 + 8, node:],
-                        ],
-                        axis=0,
-                    )
+                    jnp.concatenate([nearby[s, at, :node], nearby[s, at, node:]], axis=0)
                     for s in range(slots - 1)
                 ],
                 axis=1,
             ).astype(BF16)
-            coupled = partial[at, :] + products(group, left, 1, slots)
+            coupled = partial[at, :] + products(group * 4, left, 1, slots)
             surface[at, :] = (source[at, :] - coupled) * scale[at, :]
-            if group % 2 == 1:
-                store(1 - slot, group * 8 - 8, 16)
-            if group == rows // 16 - 1:
-                send(1 - slot, 0, more)
-            if group == rows // 8 - 1:
-                send(1 - slot, 1, more)
+            if turn % 2 == 1:
+                store(1 - slot, pl.multiple_of(group * 8 - 8, 16), 16)
+            if turn == count // 2 - 1:
+                send(1 - slot, outer, more)
+            if turn == count - 1:
+                send(1 - slot, inner, more)
 
     def step(t, carry):
         def two(j, carry):
@@ -214,9 +216,10 @@
 
     def cells(c, carry):
         at = pl.ds(pl.multiple_of(c * 8, 8), 8)
+        span = pl.ds(pl.multiple_of(c * 8 * node, 8 * node), 8 * node)
         totals = [jnp.zeros((8, node), F32)] * 2
         for k in range(nodes_ref.shape[0]):
-            index = nodes_ref[k, at, :]
+            index = nodes_ref[k, span].reshape(8, node)
             row, lane = index // node, index % node
             found = [jnp.zeros((8, node), F32)] * 2
             for r in range(rows):
@@ -226,13 +229,13 @@
                         jnp.broadcast_to(table_ref[f, r : r + 1, :], (8, node)), lane, axis=1
                     )
                     found[f] = jnp.where(hit, picked, found[f])
-            weight = weights_ref[k, at, :]
+            weight = weights_ref[k, span].reshape(8, node)
             totals = [total + weight * value for total, value in zip(totals, found)]
         level_ref[at, :] = totals[0]
         final_ref[at, :] = totals[1]
         return carry
 
-    lax.fori_loop(0, nodes_ref.shape[1] // 8, cells, 0)
+    lax.fori_loop(0, nodes_ref.shape[1] // (8 * node), cells, 0)
 
 
 def local(domains, eta_start, forcing, diagonal, coupling, neighbours, wet, grid_nodes, grid_weights):
@@ -243,13 +246,19 @@
     fields = pl.pallas_call(
         functools.partial(surge_kernel, domains),
         out_shape=jax.ShapeDtypeStruct((2, rows, node), F32),
-        in_specs=[vmem] * 5 + [pl.BlockSpec(memory_space=pl.ANY)],
+        in_specs=[pl.BlockSpec(memory_space=pl.ANY)] * 6,
         out_specs=vmem,
         scratch_shapes=[
+            pltpu.VMEM(eta_start.shape, F32),
+            pltpu.VMEM(forcing.shape, F32),
+            pltpu.VMEM(diagonal.shape, F32),
+            pltpu.VMEM(neighbours.shape, jnp.int32),
+            pltpu.VMEM(wet.shape, jnp.int32),
             pltpu.VMEM(coupling.shape, BF16),
             pltpu.VMEM((rows // 2, slots * node, 2 * node), BF16),
             pltpu.VMEM((2, 2 * rows, 2 * node), BF16),
             pltpu.VMEM(((slots - 1) * rows, 2 * rows), BF16),
+            pltpu.VMEM((slots - 1, rows, 2 * node), F32),
             pltpu.VMEM((rows, node), F32),
             pltpu.VMEM((rows, node), F32),
             pltpu.VMEM((rows, node), F32),
@@ -257,6 +266,7 @@
             pltpu.VMEM((rows, node), F32),
             pltpu.VMEM((domains, 2 * share, node), F32),
             pltpu.VMEM((domains, 2 * share, node), F32),
+            pltpu.SemaphoreType.DMA((5,)),
             pltpu.SemaphoreType.DMA((rows // 8,)),
             pltpu.SemaphoreType.DMA((2, 2)),
             pltpu.SemaphoreType.DMA((2, 2)),
@@ -264,17 +274,16 @@
             pltpu.SemaphoreType.DMA((domains,)),
         ],
         compiler_params=pltpu.CompilerParams(
-            collective_id=0, has_side_effects=True, vmem_limit_bytes=40 << 20
+            collective_id=0, has_side_effects=True, vmem_limit_bytes=56 << 20
         ),
     )(eta_start, forcing, diagonal, neighbours, wet, coupling)
     cells = grid_nodes.shape[1]
-    shaped = (grid_nodes.shape[0], cells // node, node)
     level, final = pl.pallas_call(
         grid_kernel,
         out_shape=[jax.ShapeDtypeStruct((cells // node, node), F32)] * 2,
         in_specs=[vmem] * 3,
         out_specs=[vmem] * 2,
-    )(fields, grid_nodes.reshape(shaped), grid_weights.reshape(shaped))
+    )(fields, grid_nodes, grid_weights)
     return level.reshape(-1), final.reshape(-1)
 
 

time: 145 us -> 130 us (0.90)
  local copies, waits for them, and re-layouts: 9.22 us -> 1.38 us
  Pallas kernels: 134 us -> 127 us
    unnamed x19 -> x1, local copies, waits for them, and re-layouts: 9.22 us -> 1.38 us
    pallas_call x1, Pallas kernels: 129 us -> 122 us  [local(): pl.pallas_call(functools.partial(surge_kernel, domains), out_shape=jax.Sh...]
where the time goes in v2:
time: 130 us; the launch traced here: 129 us
  Pallas kernels  127 us (98%)
  local copies, waits for them, and re-layouts  1.38 us (1%)
    pallas_call x1, Pallas kernels, local(): pl.pallas_call(functools.partial(surge_kernel, domains), out_shape=jax.Sh...  122 us
    pallas_call x1, Pallas kernels, local(): pl.pallas_call(grid_kernel, out_shape=[jax.ShapeDtypeStruct((cells // nod...  5.57 us

profile of v2, /device:TPU:0, one launch (start us, length us, event | category | flops | bytes accessed | tf_op | source)
XLA Modules:
  0.0 129.5 jit_solution(8687784323970144419)
XLA Ops:
  0.6 1.4 %copy.10.nb_hbm = s32[64,4]{1,0:T(8,128)} copy(s32[64,4]{0,1:T(4,128)} %param.12) | data formatting | bytes 2048 | tf_op args[4]
  2.0 121.9 %shard_map.95.table_ref = f32[2,64,128]{2,1,0:T(8,128)} custom-call(f32[64,128]{1,0:T(8,128)} %eta_hbm.1, f32[4,64,128]{2,1,0:T(8,128)} %forcing_hbm.1, f32[64,128]{1,0:T(8,128)} %diag_hbm.1, s32[64,4]{1,0:T(8,128)} %copy.10.nb_hbm, s32[64,128]{1,0:T(8,128)} %wet_hbm.1, bf16[64,4,128,128]{3,2,1,0:T(8,128)(2,1)} %coupling_ref.1), custom_call_target="tpu_custom_call" | custom-call | tf_op jit(solution)/shard_map/pallas_call | solution.py:246
  123.9 5.6 %shard_map.96 = (f32[64,128]{1,0:T(8,128)}, f32[64,128]{1,0:T(8,128)}) custom-call(f32[2,64,128]{2,1,0:T(8,128)} %shard_map.95.table_ref, s32[3,8192]{1,0:T(4,128)} %nodes_ref.1, f32[3,8192]{1,0:T(4,128)} %weights_ref.1), custom_call_target="tpu_custom_call" | custom-call | tf_op jit(solution)/shard_map/pallas_call | solution.py:281

commit v3 on v2

--- a/solution.py
+++ b/solution.py
@@ -16,7 +16,7 @@
     domains,
     eta_hbm, forcing_hbm, diag_hbm, nb_hbm, wet_hbm, coupling_ref,
     out_ref,
-    eta_ref, forcing_ref, diag_ref, nb_ref, wet_ref, raw, weights, padded, onehot, nearby, surface, source, scale, highest, partial, sending, landing,
+    eta_ref, forcing_ref, diag_ref, nb_ref, wet_ref, raw, weights, padded, onehot, surface, source, scale, highest, partial, sending, landing,
     small_sem, load_sem, send_sem, recv_sem, strip_send, strip_recv,
 ):
     steps, rows, node = forcing_ref.shape
@@ -59,18 +59,22 @@
     for load in small:
         load.wait()
     scale[...] = wet_ref[...].astype(F32) / diag_ref[...]
-    lane = lax.broadcasted_iota(jnp.int32, (rows, 2 * rows), 1)
+    place = lax.broadcasted_iota(jnp.int32, (2 * rows, rows), 0)
     for s in range(1, slots):
-        onehot[(s - 1) * rows : s * rows, :] = (nb_ref[:, s : s + 1] == lane).astype(F32).astype(BF16)
+        match = (nb_ref[s : s + 1, :] == place).astype(F32)
+        match = jnp.concatenate([match, match], axis=1).T.astype(BF16)
+        for half in range(2):
+            onehot[half, (s - 1) * margin : s * margin, :] = match[half * margin : (half + 1) * margin]
 
     def split(value):
         high = value.astype(BF16).astype(F32)
         return high, value - high
 
-    def store(slot, row, count):
-        high, low = split(surface[pl.ds(row, count), :])
-        padded[slot, pl.ds(margin + row, count), :node] = high.astype(BF16)
-        padded[slot, pl.ds(margin + row, count), node:] = low.astype(BF16)
+    def store(slot, row, value):
+        at = pl.ds(pl.multiple_of(margin + row, margin), value.shape[0])
+        high, low = split(value)
+        padded[slot, at, :node] = high.astype(BF16)
+        padded[slot, at, node:] = low.astype(BF16)
 
     def exchange(slot, side, step):
         return pltpu.make_async_remote_copy(
@@ -95,12 +99,16 @@
         @pl.when(present(side))
         def _():
             exchange(slot, 1 - side, -1).wait_recv()
+
+    def sent(slot, side, condition):
+        @pl.when(jnp.logical_and(present(side), condition))
+        def _():
             exchange(slot, side, 1).wait_send()
 
     surface[...] = eta_ref[...]
     source[...] = diag_ref[...] * eta_ref[...] + forcing_ref[0]
     highest[...] = jnp.full((rows, node), -jnp.inf, F32)
-    store(0, 0, rows)
+    store(0, 0, eta_ref[...])
 
     pl.semaphore_wait(barrier, domains - 1)
     send(0, outer, True)
@@ -133,7 +141,9 @@
             result = jnp.where(sub == 2 * q + 1, both[:, node:], result)
         return result
 
-    def sweep(slot, more):
+    def sweep(slot, later, more):
+        sent(1 - slot, inner, later)
+        sent(1 - slot, outer, later)
         for group in range(rows // 8):
             at = slice(group * 8, group * 8 + 8)
             left = jnp.concatenate(split(surface[at, :]), axis=0).astype(BF16)
@@ -141,33 +151,29 @@
 
         receive(slot, inner)
         receive(slot, outer)
-        near = jnp.dot(onehot[...], padded[slot], preferred_element_type=F32)
-        for s in range(slots - 1):
-            nearby[s] = near[s * rows : (s + 1) * rows, :]
-        count = rows // 8
-        for turn in range(count):
-            group = turn + (outer if turn < count // 2 else -outer) * (count // 2)
-            at = pl.ds(pl.multiple_of(group * 8, 8), 8)
-            left = jnp.concatenate(
-                [
-                    jnp.concatenate([nearby[s, at, :node], nearby[s, at, node:]], axis=0)
-                    for s in range(slots - 1)
-                ],
-                axis=1,
-            ).astype(BF16)
-            coupled = partial[at, :] + products(group * 4, left, 1, slots)
-            surface[at, :] = (source[at, :] - coupled) * scale[at, :]
-            if turn % 2 == 1:
-                store(1 - slot, pl.multiple_of(group * 8 - 8, 16), 16)
-            if turn == count // 2 - 1:
-                send(1 - slot, outer, more)
-            if turn == count - 1:
-                send(1 - slot, inner, more)
+        count = margin // 8
+        known = padded[slot]
+        for half in (outer, inner):
+            near = jnp.dot(onehot[half], known, preferred_element_type=F32)
+            at = pl.ds(pl.multiple_of(half * margin, margin), margin)
+            coupled = []
+            for turn in range(count):
+                parts = [
+                    near[s * margin + turn * 8 : s * margin + turn * 8 + 8] for s in range(slots - 1)
+                ]
+                left = jnp.concatenate(
+                    [jnp.concatenate([part[:, :node], part[:, node:]], axis=0) for part in parts], axis=1
+                ).astype(BF16)
+                coupled.append(products(half * (margin // 2) + turn * 4, left, 1, slots))
+            fresh = (source[at, :] - (partial[at, :] + jnp.concatenate(coupled, axis=0))) * scale[at, :]
+            surface[at, :] = fresh
+            store(1 - slot, half * margin, fresh)
+            send(1 - slot, half, more)
 
     def step(t, carry):
         def two(j, carry):
-            sweep(0, True)
-            sweep(1, jnp.logical_or(t < steps - 1, j < SWEEPS // 2 - 1))
+            sweep(0, jnp.logical_or(t > 0, j > 0), True)
+            sweep(1, True, jnp.logical_or(t < steps - 1, j < SWEEPS // 2 - 1))
             return carry
 
         lax.fori_loop(0, SWEEPS // 2, two, 0)
@@ -177,6 +183,8 @@
         return carry
 
     lax.fori_loop(0, steps, step, 0)
+    sent(1, inner, True)
+    sent(1, outer, True)
 
     for q in range(domains):
         sending[q, :share, :] = highest[q * share : (q + 1) * share, :]
@@ -252,13 +260,12 @@
             pltpu.VMEM(eta_start.shape, F32),
             pltpu.VMEM(forcing.shape, F32),
             pltpu.VMEM(diagonal.shape, F32),
-            pltpu.VMEM(neighbours.shape, jnp.int32),
+            pltpu.VMEM(neighbours.shape[::-1], jnp.int32),
             pltpu.VMEM(wet.shape, jnp.int32),
             pltpu.VMEM(coupling.shape, BF16),
             pltpu.VMEM((rows // 2, slots * node, 2 * node), BF16),
             pltpu.VMEM((2, 2 * rows, 2 * node), BF16),
-            pltpu.VMEM(((slots - 1) * rows, 2 * rows), BF16),
-            pltpu.VMEM((slots - 1, rows, 2 * node), F32),
+            pltpu.VMEM((2, (slots - 1) * rows // 2, 2 * rows), BF16),
             pltpu.VMEM((rows, node), F32),
             pltpu.VMEM((rows, node), F32),
             pltpu.VMEM((rows, node), F32),
@@ -276,7 +283,7 @@
         compiler_params=pltpu.CompilerParams(
             collective_id=0, has_side_effects=True, vmem_limit_bytes=56 << 20
         ),
-    )(eta_start, forcing, diagonal, neighbours, wet, coupling)
+    )(eta_start, forcing, diagonal, neighbours.T, wet, coupling)
     cells = grid_nodes.shape[1]
     level, final = pl.pallas_call(
         grid_kernel,

time: 130 us -> 127 us (0.977)
  local copies, waits for them, and re-layouts: 1.38 us -> 0 us
    unnamed x1 -> x0, local copies, waits for them, and re-layouts: 1.38 us -> none
where the time goes in v3:
time: 127 us
  Pallas kernels  127 us (100%)
    pallas_call x1, Pallas kernels, local(): pl.pallas_call(functools.partial(surge_kernel, domains), out_shape=jax.Sh...  121 us
    pallas_call x1, Pallas kernels, local(): pl.pallas_call(grid_kernel, out_shape=[jax.ShapeDtypeStruct((cells // nod...  5.57 us

profile of v3, /device:TPU:0, one launch (start us, length us, event | category | flops | bytes accessed | tf_op | source)
XLA Modules:
  0.0 127.3 jit_solution(6248855369510347047)
XLA Ops:
  0.6 121.1 %shard_map.95.table_ref = f32[2,64,128]{2,1,0:T(8,128)} custom-call(f32[64,128]{1,0:T(8,128)} %eta_hbm.1, f32[4,64,128]{2,1,0:T(8,128)} %forcing_hbm.1, f32[64,128]{1,0:T(8,128)} %diag_hbm.1, s32[4,64]{1,0:T(4,128)} %bitcast.3, s32[64,128]{1,0:T(8,128)} %wet_hbm.1, bf16[64,4,128,128]{3,2,1,0:T(8,128)(2,1)} %coupling_ref.1), custom_call_target="tpu_custom_call" | custom-call | tf_op jit(solution)/shard_map/pallas_call | solution.py:254
  121.7 5.6 %shard_map.96 = (f32[64,128]{1,0:T(8,128)}, f32[64,128]{1,0:T(8,128)}) custom-call(f32[2,64,128]{2,1,0:T(8,128)} %shard_map.95.table_ref, s32[3,8192]{1,0:T(4,128)} %nodes_ref.1, f32[3,8192]{1,0:T(4,128)} %weights_ref.1), custom_call_target="tpu_custom_call" | custom-call | tf_op jit(solution)/shard_map/pallas_call | solution.py:288
